TPU v7x, 256 devices: a whole 4x4x8 slice. The times are simulated.
256 devices in a mesh: fsdp: 16 (over x_lo, y, core), group: 8 (over z), dp: 2 (over x_hi).
Axes of the slice: x: 4 (x_hi: 2, x_lo: 2; x = x_hi * 2 + x_lo), y: 4, z: 8, core: 2. Of those that a mesh axis runs over, the one named last changes fastest.
Arguments:
- hidden_states: bfloat16 [32, 16, 256, 5120], P(('fsdp', 'dp'), 'group'), may hold values from -6 to 6
- kv_weight: bfloat16 [5120, 1024], P('fsdp'), may hold values from -0.078125 to 0.078125
- sensitivity: bfloat16 [32, 16, 256, 1024], P(('fsdp', 'dp'), 'group'), may hold values from -6 to 6
- logp_shift: float32 [32, 16, 256], P(('fsdp', 'dp'), 'group'), may hold values from -0.6 to 0.6
- token_mask: int32 [32, 16, 256], P(('fsdp', 'dp'), 'group'), may hold values 0 or 1
- lengths: int32 [32, 16], P(('fsdp', 'dp'), 'group'), may hold values from 64 to 256
- rewards: int32 [32, 16], P(('fsdp', 'dp'), 'group'), may hold values from 0 to 100
Outputs:
- kv_grad: float32 [5120, 1024], P('fsdp', 'group')
All inputs are finite; a program needn't handle non-finite values. No bound on the sum of `token_mask` on one device may be relied on, other than what follows from the above.
Results may differ from a plain program's by a relative error of at most 0.0029.
Values may be sent and summed in bfloat16 or wider, within the bound.
No kernel may reach another device: no remote copies, remote signals or barrier semaphores. Data moves between devices by JAX's collectives and lax.ppermute only.
A program may use at most 128 MiB of HBM per device.

v0:
```python
import math

import jax
import jax.numpy as jnp
from jax import lax
from jax.sharding import PartitionSpec as P

GROUP_SIZE = 16


CLIP_LOW = 0.8
CLIP_HIGH = 1.28
LOSS_SCALE = 64.0


def shards(hidden_states, kv_weight, sensitivity, logp_shift, token_mask, lengths, rewards):
    seq_slots = hidden_states.shape[2]
    model_width = hidden_states.shape[3]
    kv_columns = kv_weight.shape[1]
    scale_read = 0.3 / math.sqrt(kv_columns)
    token_rows = hidden_states.reshape(-1, model_width)
    sens_rows = sensitivity.reshape(-1, kv_columns)
    columns = token_rows
    projected = jnp.dot(
        columns,
        lax.all_gather(kv_weight, "fsdp", axis=0, tiled=True),
        preferred_element_type=jnp.float32,
    )
    reward_vals = rewards.astype(jnp.float32)
    reward_sum, squares = lax.psum(
        (jnp.sum(reward_vals, axis=1), jnp.sum(reward_vals * reward_vals, axis=1)), "group"
    )
    reward_mean = reward_sum / GROUP_SIZE
    spread = jnp.sqrt(jnp.maximum(squares / GROUP_SIZE - reward_mean * reward_mean, 0.0))
    advantage = (reward_vals - reward_mean[:, None]) / jnp.maximum(spread, 1.0)[:, None]
    positions = lax.broadcasted_iota(jnp.int32, (1, 1, seq_slots), 2)
    kept = ((positions < lengths[:, :, None]) & (token_mask == 1)).astype(jnp.float32)
    coef = -LOSS_SCALE * advantage[:, :, None] * kept / lengths[:, :, None].astype(jnp.float32)
    linear = scale_read * jnp.sum(projected * sens_rows.astype(jnp.float32), axis=1)
    ratios = jnp.exp(logp_shift.reshape(-1) + linear)
    factor = jnp.clip(ratios, CLIP_LOW, CLIP_HIGH) * coef.reshape(-1) * scale_read
    step_dir = (factor[:, None] * sens_rows.astype(jnp.float32)).astype(jnp.bfloat16)
    columns = token_rows
    row_block = lax.psum_scatter(
        lax.dot_general(
            columns, step_dir, (((0,), (0,)), ((), ())), preferred_element_type=jnp.float32
        ),
        "fsdp",
        scatter_dimension=0,
        tiled=True,
    )
    owned_grad = lax.psum_scatter(row_block, "group", scatter_dimension=1, tiled=True)
    return lax.psum(owned_grad, "dp")


def solution(mesh):
    in_specs = (
        P(("fsdp", "dp"), "group", None, None),
        P("fsdp", None),
        P(("fsdp", "dp"), "group", None, None),
        P(("fsdp", "dp"), "group", None),
        P(("fsdp", "dp"), "group", None),
        P(("fsdp", "dp"), "group"),
        P(("fsdp", "dp"), "group"),
    )
    out_specs = P("fsdp", "group")
    return jax.shard_map(shards, mesh=mesh, in_specs=in_specs, out_specs=out_specs, check_vma=False)
```

profile of v0, /device:TPU:2, one launch (start us, length us, event | category | flops | bytes accessed | tf_op | source)
XLA Modules:
  0.0 330.2 jit_solution(14021741094160121561)
XLA Ops:
  6.5 0.0 all-gather.2.cloned.1.call-start
  6.5 0.7 all-gather.2.cloned.1.call-update
  7.3 0.0 reduce-scatter.7.cloned.1.call-start
  7.3 1.3 convert_reduce_fusion
  8.6 20.7 %all-reduce = (f32[1]{0:T(128)}, f32[1]{0:T(128)}) all-reduce(f32[1]{0:T(128)} %bitcast.6, f32[1]{0:T(128)} %bitcast.4), channel_id=1, replica_groups=mesh['fsdp'=16,'group'=8,'dp'=2] {'group'}, use_global_device_ids=true, to_apply=%region_4.0 | all-reduce | flops 2 | bytes 16 | tf_op jit(solution)/shard_map/psum | solution.py:30
  31.9 0.7 bitcast_convert_fusion
  32.6 0.7 multiply_bitcast_fusion
  33.2 43.4 %all-gather.2.cloned.1.call-done = bf16[5120,1024]{1,0:T(8,128)(2,1)} async-done(((bf16[320,1024]{1,0:T(8,128)(2,1)}), bf16[5120,1024]{1,0:T(8,128)(2,1)}) %all-gather.2.cloned.1.call-update) | async-done | bytes 10485776 | tf_op jit(solution)/shard_map/all_gather | solution.py:26
  76.6 0.0 copy-start.1
  76.6 0.0 copy-start.2
  76.6 0.0 copy-start.3
  76.6 0.0 copy-start
  76.6 10.2 %fusion.1 = f32[512]{0:T(512)S(1)} fusion(bf16[512,5120]{1,0:T(8,128)(2,1)} %bitcast.38, bf16[5120,1024]{1,0:T(8,128)(2,1)} %all-gather.2.cloned.1.call-done, bf16[1,2,256,1024]{3,2,1,0:T(8,128)(2,1)} %param.9), kind=kOutput, calls=%fused_computation.3 | convolution fusion | flops 5370281472 | bytes 16779264 | tf_op jit(solution)/shard_map/dot_general | solution.py:24
  86.9 0.0 copy-done.1
  86.9 0.0 copy-done.2
  86.9 0.0 copy-done.3
  86.9 0.1 fusion.7
  87.0 0.0 copy-done
  87.0 12.5 %convolution_bitcast_fusion = f32[5120,1024]{0,1:T(8,128)} fusion(bf16[1,2,256,5120]{3,2,1,0:T(8,128)(2,1)} %param.7, f32[2,256]{1,0:T(2,128)S(1)} %fusion.7, bf16[1,2,256,1024]{3,2,1,0:T(8,128)(2,1)S(1)} %copy-done), kind=kOutput, calls=%fused_computation | convolution fusion | flops 5370281984 | bytes 27265024 | tf_op jit(solution)/shard_map/dot_general | solution.py:45
  99.4 21.3 %copy.13 = f32[5120,1024]{1,0:T(8,128)} copy(f32[5120,1024]{0,1:T(8,128)} %convolution_bitcast_fusion) | data formatting | bytes 41943040
  120.8 0.0 reduce-scatter.7.cloned.1.call-update
  120.8 0.0 reduce-scatter.5.cloned.1.call-start
  120.8 122.4 %reduce-scatter.7.cloned.1.call-done = f32[320,1024]{1,0:T(8,128)} async-done(((f32[5120,1024]{1,0:T(8,128)}), f32[320,1024]{1,0:T(8,128)}) %reduce-scatter.7.cloned.1.call-update) | async-done | bytes 1310736
  243.2 2.9 copy.14
  246.1 0.0 reduce-scatter.5.cloned.1.call-update
  246.2 0.0 all-reduce.3.cloned.1.call-start
  246.2 40.0 %reduce-scatter.5.cloned.1.call-done = f32[320,128]{0,1:T(8,128)} async-done(((f32[320,1024]{0,1:T(8,128)}), f32[320,128]{0,1:T(8,128)}) %reduce-scatter.5.cloned.1.call-update) | async-done | bytes 163856 | tf_op jit(solution)/shard_map/reduce_scatter | solution.py:52
  286.2 0.0 all-reduce.3.cloned.1.call-update
  286.3 35.7 %all-reduce.3.cloned.1.call-done = f32[320,128]{0,1:T(8,128)} async-done(((f32[320,128]{0,1:T(8,128)}), f32[320,128]{0,1:T(8,128)}) %all-reduce.3.cloned.1.call-update) | async-done | bytes 163856 | tf_op jit(solution)/shard_map/psum | solution.py:53
  322.0 1.7 copy.11
  (2 shorter events, 0.0 us)
Async XLA Ops:
  6.5 70.1 %all-gather.2.cloned.1.call-start = ((), (), s32[]{:S(2)}) async-start(), calls=%async_computation.2 | async-start | bytes 11141120 | tf_op jit(solution)/shard_map/all_gather | solution.py:26
  7.3 235.9 %reduce-scatter.7.cloned.1.call-start = ((), (), s32[]{:S(2)}) async-start(), calls=%async_computation.5 | async-start | bytes 22282240
  76.6 10.2 %copy-start.1 = (f32[1,2,256]{2,1,0:T(2,128)S(1)}, f32[1,2,256]{2,1,0:T(2,128)}, u32[]{:S(2)}) copy-start(f32[1,2,256]{2,1,0:T(2,128)} %param.10) | copy-start | bytes 6148
  76.6 10.2 %copy-start.2 = (s32[1,2,256]{2,1,0:T(2,128)S(1)}, s32[1,2,256]{2,1,0:T(2,128)}, u32[]{:S(2)}) copy-start(s32[1,2,256]{2,1,0:T(2,128)} %param.11) | copy-start | bytes 6148
  76.6 10.2 %copy-start.3 = (s32[1,2]{1,0:T(1,128)S(1)}, s32[1,2]{1,0:T(1,128)}, u32[]{:S(2)}) copy-start(s32[1,2]{1,0:T(1,128)} %param.12) | copy-start | bytes 28
  76.6 10.3 %copy-start = (bf16[1,2,256,1024]{3,2,1,0:T(8,128)(2,1)S(1)}, bf16[1,2,256,1024]{3,2,1,0:T(8,128)(2,1)}, u32[]{:S(2)}) copy-start(bf16[1,2,256,1024]{3,2,1,0:T(8,128)(2,1)} %param.9) | copy-start | bytes 3145732
  120.8 165.5 %reduce-scatter.5.cloned.1.call-start = ((), (), s32[]{:S(2)}) async-start(), calls=%async_computation.3 | async-start | bytes 1769472 | tf_op jit(solution)/shard_map/reduce_scatter | solution.py:52
  246.2 75.8 %all-reduce.3.cloned.1.call-start = ((), (), s32[]{:S(2)}) async-start(), calls=%async_computation.4 | async-start | bytes 393216 | tf_op jit(solution)/shard_map/psum | solution.py:53
Sparse Core Ops, SparseCore 0:
  9.2 67.3 all-gather.1
  120.9 122.2 reduce-scatter.6
  246.3 39.9 reduce-scatter.4
  288.7 33.2 all-reduce.2
where the time goes:
time: 332 us; the launch traced here: 330 us
  waiting for transfers between devices  242 us (73%)
  local copies, waits for them, and re-layouts  26 us (8%)
  matrix products  22.7 us (7%)
  blocking collectives  20.7 us (6%)
  between operations  15.8 us (5%)
    unnamed x5, waiting for transfers between devices  123 us
    all_gather x1, waiting for transfers between devices, shards(): lax.all_gather(kv_weight, 'fsdp', axis=0, tiled=True)  43.4 us
    reduce_scatter x1, waiting for transfers between devices, shards(): lax.psum_scatter(row_block, 'group', scatter_dimension=1, tiled=True)  40 us
    psum x1, waiting for transfers between devices, shards(): return lax.psum(owned_grad, 'dp')  35.7 us
    unnamed x10, local copies, waits for them, and re-layouts  24.3 us
    psum x1, blocking collectives, shards(): lax.psum((jnp.sum(reward_vals, axis=1), jnp.sum(reward_vals * reward_vals...  20.7 us
    dot_general x1, matrix products, shards(): lax.dot_general(columns, step_dir, (((0,), (0,)), ((), ())), preferred_el...  12.5 us
    dot_general x1, matrix products, shards(): jnp.dot(columns, lax.all_gather(kv_weight, 'fsdp', axis=0, tiled=True), p...  10.2 us
  transfers between devices with their start and end apart: 4, of which 4 were waited for; matrix products, arithmetic and copies ran while one was open for 1% of the time, Pallas kernels for 0%

commit v1 on v0

v1 whole, which is shorter than its diff:
```python
import functools
import math

import jax
import jax.numpy as jnp
from jax import lax
from jax.experimental import pallas as pl
from jax.experimental.pallas import tpu as pltpu
from jax.sharding import PartitionSpec as P

GROUP_SIZE = 16
CLIP_LOW = 0.8
CLIP_HIGH = 1.28
LOSS_SCALE = 64.0

NX, NY, NC, NZ, NDP = 2, 4, 2, 8, 2
PLANE = [(x, y, c) for x in range(NX) for y in range(NY) for c in range(NC)]


def place(x, y, c):
    return (x * NY + y % NY) * NC + c


def ring_x(x, y, c, dp, hop):
    ring = (dp * NX + x + hop) % (NX * NDP)
    return place(ring % NX, y, c) * NDP + ring // NX


OTHER_CORE = [(place(x, y, c), place(x, y, 1 - c)) for x, y, c in PLANE]


def to_core(a):
    return lax.ppermute(a, "fsdp", OTHER_CORE)


def along_y(a, way):
    pairs = [(place(x, y, c), place(x, y + (way if c == 0 else -way), c)) for x, y, c in PLANE]
    return lax.ppermute(a, "fsdp", pairs)


def rows_along_y(a, way):
    pairs = []
    for x, y, c in PLANE:
        for z in range(NZ):
            owner = (c + z) % NC
            far_y = y + (1 if c == 0 else -1)
            ends = place(x, y, c) * NZ + z, place(x, far_y, owner) * NZ + z
            pairs.append(ends if way > 0 else ends[::-1])
    return lax.ppermute(a, ("fsdp", "group"), pairs)


def along_z(a):
    pairs = []
    for x, y, c in PLANE:
        for z in range(NZ):
            to = z ^ 1 if c == 0 else (z + (1 if z % 2 else -1)) % NZ
            pairs.append((place(x, y, c) * NZ + z, place(x, y, c) * NZ + to))
    return lax.ppermute(a, ("fsdp", "group"), pairs)


def along_x(a, way):
    pairs = [
        (place(x, y, c) * NDP + dp, ring_x(x, y, c, dp, way if c == 0 else -way))
        for x, y, c in PLANE
        for dp in range(NDP)
    ]
    return lax.ppermute(a, ("fsdp", "dp"), pairs)


def to_z_xor(a, bit):
    return lax.ppermute(a, "group", [(z, z ^ bit) for z in range(NZ)])


def to_z(a, hop):
    return lax.ppermute(a, "group", [(z, (z + hop) % NZ) for z in range(NZ)])


def to_dp(a):
    return lax.ppermute(a, "dp", [(0, 1), (1, 0)])


def after(a, earlier):
    return lax.optimization_barrier((a, earlier))[0]


def after(a, earlier):
    return lax.optimization_barrier((a, earlier))[0]


def read_kernel(count, spots, mine, theirs, sens_mine, sens_theirs, *refs):
    blocks, (before, after_, *hids), (padded, sems) = refs[:count], refs[count : count + 2 + count], refs[-2:]
    rows = blocks[0].shape[0]
    window = hids[0].shape[1]
    spare = window - rows
    tokens = mine.shape[0]
    copies = []
    for i in range(count):
        start = pl.multiple_of(spots[2 * i] * 128, 128)
        offset = pl.multiple_of(spots[2 * i + 1] * spare, spare)
        padded[i, :spare] = jnp.zeros((spare, padded.shape[2]), padded.dtype)
        padded[i, rows:] = jnp.zeros((spare, padded.shape[2]), padded.dtype)
        moves = (
            (blocks[i], padded.at[i, pl.ds(offset, rows)]),
            (mine.at[:, pl.ds(start, window)], hids[i].at[pl.ds(0, tokens)]),
            (theirs.at[:, pl.ds(start, window)], hids[i].at[pl.ds(tokens, tokens)]),
        )
        copies.append([pltpu.make_async_copy(src, dst, sems.at[i, j]) for j, (src, dst) in enumerate(moves)])
        for copy in copies[-1]:
            copy.start()
    after_[...] = before[...]
    chunk = 256
    for i in range(count):
        for copy in copies[i]:
            copy.wait()
        for at in range(0, 2 * tokens, chunk):
            sens = sens_mine if at < tokens else sens_theirs
            part = jnp.dot(hids[i][at : at + chunk], padded[i], preferred_element_type=jnp.float32)
            part = part * sens[at % tokens : at % tokens + chunk].astype(jnp.float32)
            total = after_[at : at + chunk]
            for lane in range(0, part.shape[1], 128):
                total = total + part[:, lane : lane + 128]
            after_[at : at + chunk] = total


def read_blocks(spots, mine, theirs, sens_mine, sens_theirs, blocks, before):
    count = len(blocks)
    rows, columns = blocks[0].shape
    window = -(-rows // 128) * 128
    tokens = 2 * mine.shape[0]
    vmem = pl.BlockSpec(memory_space=pltpu.VMEM)
    whole = pl.BlockSpec(memory_space=pl.ANY)
    hid = jax.ShapeDtypeStruct((tokens, window), mine.dtype)
    return pl.pallas_call(
        functools.partial(read_kernel, count),
        in_specs=[pl.BlockSpec(memory_space=pltpu.SMEM), whole, whole, vmem, vmem] + [whole] * count + [vmem],
        out_specs=[vmem] * (1 + count),
        out_shape=[jax.ShapeDtypeStruct((tokens, 128), jnp.float32)] + [hid] * count,
        scratch_shapes=[
            pltpu.VMEM((count, window, columns), mine.dtype),
            pltpu.SemaphoreType.DMA((count, 3)),
        ],
        cost_estimate=pl.CostEstimate(flops=0, bytes_accessed=0, transcendentals=0),
        compiler_params=pltpu.CompilerParams(vmem_limit_bytes=32 * 2**20),
    )(spots, mine, theirs, sens_mine, sens_theirs, *blocks, before)


def shards(hidden_states, kv_weight, sensitivity, logp_shift, token_mask, lengths, rewards):
    seq_slots = hidden_states.shape[2]
    width = hidden_states.shape[3]
    columns = kv_weight.shape[1]
    rows = kv_weight.shape[0]
    scale_read = 0.3 / math.sqrt(columns)
    at = lax.axis_index("fsdp")
    core = at % NC
    y = (at // NC) % NY
    x = at // (NC * NY)
    first = core == 0
    f32, bf16 = jnp.float32, jnp.bfloat16

    hid_mine = hidden_states.reshape(-1, width)
    hid_theirs = to_core(hid_mine)
    sens_mine = sensitivity.reshape(-1, columns)
    sens_theirs = to_core(sens_mine)
    sens = jnp.concatenate([sens_mine, sens_theirs], axis=0)
    positions = lax.broadcasted_iota(jnp.int32, (1, 1, seq_slots), 2)
    kept = ((positions < lengths[:, :, None]) & (token_mask == 1)).astype(f32)
    spread_out = lambda a: jnp.broadcast_to(a.astype(f32)[:, :, None], kept.shape).reshape(-1)
    per_token = jnp.stack([logp_shift.reshape(-1), kept.reshape(-1), spread_out(lengths), spread_out(rewards)])
    tokens = per_token.shape[1]
    token_theirs = to_core(per_token)

    kind = (core + lax.axis_index("group")) % NC
    next_y = jnp.where(first, 1, NY - 1)
    spots = {
        "own": (0, 0, core),
        "side": (1, 0, core),
        "near": (0, next_y, kind),
        "near_other": (0, next_y, 1 - kind),
        "near_side": (1, next_y, kind),
        "near_side_other": (1, next_y, 1 - kind),
        "far": (0, 2, kind),
        "far_side": (1, 2, kind),
    }
    h, w = {}, {"own": kv_weight}

    def read_terms(before, *names):
        where = []
        for name in names:
            dx, dy, owner = spots[name]
            chip = (x ^ dx) * NY + (y + dy) % NY
            where += [chip * (NC * rows // 128) + owner * (rows // 128), owner]
        total, *cut = read_blocks(
            jnp.stack(where).astype(jnp.int32), hid_mine, hid_theirs, sens_mine, sens_theirs,
            [w[name] for name in names], before,
        )
        h.update(zip(names, cut))
        return total

    w["near"] = rows_along_y(kv_weight, -1)
    w["side"] = along_x(kv_weight, -1)
    per_token = jnp.concatenate([per_token, token_theirs], axis=1)
    shift, kept, lens, reward_vals = per_token
    reward_pairs = reward_vals.reshape(NC, -1, seq_slots)[:, :, 0]
    sums = jnp.concatenate([jnp.sum(reward_pairs, axis=1), jnp.sum(reward_pairs * reward_pairs, axis=1)])
    sums = sums + to_z_xor(sums, 1)

    near, _, sums = lax.optimization_barrier((w["near"], w["side"], sums))
    w["near_other"] = along_z(near)
    w["near_side"] = along_x(near, -1)
    w["far"] = along_y(near, -1)
    sums = sums + to_z_xor(sums, 2)
    read = read_terms(jnp.zeros((2 * tokens, 128), f32), "own", "side", "near")

    near_side, far, _, sums, read = lax.optimization_barrier(
        (w["near_side"], w["far"], w["near_other"], sums, read)
    )
    w["near_side_other"] = along_z(near_side)
    w["far_side"] = along_x(far, -1)
    sums = sums + to_z_xor(sums, 4)
    reward_mean = sums[:NC] / GROUP_SIZE
    spread = jnp.sqrt(jnp.maximum(sums[NC:] / GROUP_SIZE - reward_mean * reward_mean, 0.0))
    advantage = (reward_vals.reshape(NC, -1) - reward_mean[:, None]) / jnp.maximum(spread, 1.0)[:, None]
    coef = -LOSS_SCALE * advantage.reshape(-1) * kept / lens
    read = read_terms(read, "near_other", "near_side", "far")
    coef, read = lax.optimization_barrier((coef, read))
    read = jnp.sum(read_terms(read, "near_side_other", "far_side"), axis=1)

    read_theirs = to_core(read)
    read = read + jnp.concatenate([read_theirs[tokens:], read_theirs[:tokens]])
    ratios = jnp.exp(shift + scale_read * read)
    factor = jnp.clip(ratios, CLIP_LOW, CLIP_HIGH) * coef * scale_read
    step_dir = (factor[:, None] * sens.astype(f32)).astype(bf16)

    def term(name, step):
        out = lax.dot_general(h[name], step, (((0,), (0,)), ((), ())), preferred_element_type=f32)
        return name, lax.optimization_barrier(out)

    def add(named, *received):
        name, total = named
        spare = total.shape[0] - rows
        total = jnp.where(spots[name][2] == 0, total[:rows], total[spare:])
        for r in received:
            total = total + r.astype(f32)
        return total

    far_side = along_x(add(term("far_side", step_dir)).astype(bf16), 1)
    near_side_other = along_z(add(term("near_side_other", step_dir)).astype(bf16))
    far = term("far", step_dir)
    near_side = term("near_side", step_dir)
    near_other = add(term("near_other", step_dir)).astype(bf16)

    step, near_other = lax.optimization_barrier((step_dir, near_other, far_side, near_side_other))[:2]
    far = along_y(add(far, far_side).astype(bf16), 1)
    near_side = along_x(add(near_side, near_side_other).astype(bf16), 1)
    near_other = along_z(near_other)
    near = term("near", step)
    side = add(term("side", step)).astype(bf16)

    step, side = lax.optimization_barrier((step_dir, side, far, near_side, near_other))[:2]
    near = rows_along_y(add(near, near_side, far, near_other).astype(bf16), 1)
    side = along_x(side, 1)
    row_block = add(term("own", step), side, near)

    own = columns // NZ
    z = lax.axis_index("group")
    total = lax.dynamic_slice_in_dim(row_block, z * own, own, axis=1)
    narrow_block = row_block.astype(bf16)
    for hop in (4, 3, 5, 2, 6, 1, 7):
        block = lax.dynamic_slice_in_dim(narrow_block, ((z + hop) % NZ) * own, own, axis=1)
        total = total + to_z(block, hop).astype(f32)
    return total + to_dp(total)


def solution(mesh):
    in_specs = (
        P(("fsdp", "dp"), "group", None, None),
        P("fsdp", None),
        P(("fsdp", "dp"), "group", None, None),
        P(("fsdp", "dp"), "group", None),
        P(("fsdp", "dp"), "group", None),
        P(("fsdp", "dp"), "group"),
        P(("fsdp", "dp"), "group"),
    )
    out_specs = P("fsdp", "group")
    return jax.shard_map(shards, mesh=mesh, in_specs=in_specs, out_specs=out_specs, check_vma=False)
```

time: 332 us -> 141 us (0.42)
  the two profiles are of different devices: /device:TPU:2 before, /device:TPU:64 now
where the time goes in v1:
time: 141 us; the launch traced here: 140 us
  waiting for transfers between devices  54.8 us (39%)
  starting transfers between devices  38.8 us (28%)
  Pallas kernels  16.4 us (12%)
  local copies, waits for them, and re-layouts  13.4 us (10%)
  other arithmetic  8.26 us (6%)
  matrix products  8.07 us (6%)
    pallas_call x3, Pallas kernels, read_blocks(): pl.pallas_call(functools.partial(read_kernel, count), in_specs=[pl.BlockS...  16.4 us
    ppermute x7, starting transfers between devices, to_z(): return lax.ppermute(a, 'group', [(z, (z + hop) % NZ) for z in range(NZ)])  12.8 us
    ppermute x2, waiting for transfers between devices, rows_along_y(): return lax.ppermute(a, ('fsdp', 'group'), pairs)  12.6 us
    unnamed x59, local copies, waits for them, and re-layouts  12.4 us
    ppermute x7, waiting for transfers between devices, to_z(): return lax.ppermute(a, 'group', [(z, (z + hop) % NZ) for z in range(NZ)])  9.43 us
    ppermute x4, waiting for transfers between devices, along_z(): return lax.ppermute(a, ('fsdp', 'group'), pairs)  8.95 us
    dot_general x8, matrix products, term(): lax.dot_general(h[name], step, (((0,), (0,)), ((), ())), preferred_elemen...  8.07 us
    ppermute x6, waiting for transfers between devices, along_x(): return lax.ppermute(a, ('fsdp', 'dp'), pairs)  7.96 us
  transfers between devices with their start and end apart: 29, of which 17 were waited for; matrix products, arithmetic and copies ran while one was open for 9% of the time, Pallas kernels for 9%

profile of v1, /device:TPU:64, one launch (start us, length us, event | category | flops | bytes accessed | tf_op | source)
XLA Modules:
  0.0 140.1 jit_solution(2783409084487632773)
XLA Ops:
  3.5 2.8 %collective-permute-start.2 = (bf16[320,1024]{1,0:T(8,128)(2,1)}, bf16[320,1024]{1,0:T(8,128)(2,1)S(1)}, u32[]{:S(2)}, u32[]{:S(2)}) collective-permute-start(bf16[320,1024]{1,0:T(8,128)(2,1)} %refs_0_.1), channel_id=1, source_target_pairs={{0,129},{1,128},{16,144},{17,145},{32,161},{33,160},{48,176},{49,1... | collective-permute-start | bytes 1966088 | tf_op jit(solution)/shard_map/ppermute | solution.py:67
  6.3 3.0 %collective-permute-start.3 = (bf16[320,1024]{1,0:T(8,128)(2,1)}, bf16[320,1024]{1,0:T(8,128)(2,1)S(1)}, u32[]{:S(2)}, u32[]{:S(2)}) collective-permute-start(bf16[320,1024]{1,0:T(8,128)(2,1)} %refs_0_.1), channel_id=1, source_target_pairs={{32,0},{50,2},{36,4},{54,6},{40,8},{58,10},{44,12},{62,14},{112,16... | collective-permute-start | bytes 1966088 | tf_op jit(solution)/shard_map/ppermute | solution.py:49
  10.1 2.0 %collective-permute-start.5 = (f32[4]{0:T(128)S(1)}, f32[4]{0:T(128)S(1)}, u32[]{:S(2)}, u32[]{:S(2)}) collective-permute-start(f32[4]{0:T(128)S(1)} %pad_maximum_fusion.2), channel_id=1, source_target_pairs={{0,2},{2,0},{4,6},{6,4},{8,10},{10,8},{12,14},{14,12},{1,3},{3,1},... | collective-permute-start | bytes 56 | tf_op jit(solution)/shard_map/ppermute | solution.py:71
  12.2 1.5 %collective-permute-done.5 = f32[4]{0:T(128)S(1)} collective-permute-done((f32[4]{0:T(128)S(1)}, f32[4]{0:T(128)S(1)}, u32[]{:S(2)}, u32[]{:S(2)}) %collective-permute-start.5) | collective-permute-done | bytes 48 | tf_op jit(solution)/shard_map/ppermute | solution.py:71
  15.6 2.2 %collective-permute-done.3.refs_2_ = bf16[320,1024]{1,0:T(8,128)(2,1)S(1)} collective-permute-done((bf16[320,1024]{1,0:T(8,128)(2,1)}, bf16[320,1024]{1,0:T(8,128)(2,1)S(1)}, u32[]{:S(2)}, u32[]{:S(2)}) %collective-permute-start.3) | collective-permute-done | bytes 655392 | tf_op jit(solution)/shard_map/ppermute | solution.py:49
  17.7 1.4 %collective-permute-start.6 = (bf16[320,1024]{1,0:T(8,128)(2,1)S(1)}, bf16[320,1024]{1,0:T(8,128)(2,1)}, u32[]{:S(2)}, u32[]{:S(2)}) collective-permute-start(bf16[320,1024]{1,0:T(8,128)(2,1)S(1)} %collective-permute-done.3.refs_2_), channel_id=1, source_target_pairs={{0,129},{1,128},{16,144},{17,145},{32,161},{33,160},{48,176},{49,1... | collective-permute-start | bytes 1966088 | tf_op jit(solution)/shard_map/ppermute | solution.py:67
  19.2 3.0 %collective-permute-start.7 = (bf16[320,1024]{1,0:T(8,128)(2,1)S(1)}, bf16[320,1024]{1,0:T(8,128)(2,1)}, u32[]{:S(2)}, u32[]{:S(2)}) collective-permute-start(bf16[320,1024]{1,0:T(8,128)(2,1)S(1)} %collective-permute-done.3.refs_2_), channel_id=1, source_target_pairs={{0,96},{16,48},{32,0},{48,80},{64,32},{80,112},{96,64},{112,16},{1... | collective-permute-start | bytes 1966088 | tf_op jit(solution)/shard_map/ppermute | solution.py:38
  22.2 4.4 %collective-permute-done.9 = f32[4]{0:T(128)S(1)} collective-permute-done((f32[4]{0:T(128)S(1)}, f32[4]{0:T(128)S(1)}, u32[]{:S(2)}, u32[]{:S(2)}) %collective-permute-start.9) | collective-permute-done | bytes 48 | tf_op jit(solution)/shard_map/ppermute | solution.py:71
  26.6 2.0 %collective-permute-start.8 = (bf16[320,1024]{1,0:T(8,128)(2,1)S(1)}, bf16[320,1024]{1,0:T(8,128)(2,1)}, u32[]{:S(2)}, u32[]{:S(2)}) collective-permute-start(bf16[320,1024]{1,0:T(8,128)(2,1)S(1)} %collective-permute-done.3.refs_2_), channel_id=1, source_target_pairs={{0,2},{2,0},{4,6},{6,4},{8,10},{10,8},{12,14},{14,12},{16,30},{18,... | collective-permute-start | bytes 1966088 | tf_op jit(solution)/shard_map/ppermute | solution.py:58
  28.9 2.5 %copy-done = bf16[1,2,256,5120]{3,2,1,0:T(8,128)(2,1)S(1)} copy-done((bf16[1,2,256,5120]{3,2,1,0:T(8,128)(2,1)S(1)}, bf16[1,2,256,5120]{3,2,1,0:T(8,128)(2,1)}, u32[]{:S(2)}) %copy-start) | copy-done | bytes 5242904
  31.4 1.2 copy-done.2
  34.8 6.2 %shard_map.76 = (f32[1024,128]{1,0:T(8,128)S(1)}, bf16[1024,384]{1,0:T(8,128)(2,1)S(1)}, bf16[1024,384]{1,0:T(8,128)(2,1)S(1)}, bf16[1024,384]{1,0:T(8,128)(2,1)S(1)}) custom-call(s32[6]{0:T(128)S(1)} %stack.55.spots, bf16[512,5120]{1,0:T(8,128)(2,1)S(1)} %bitcast.58, bf16[512,5120]{1,0:T(8,128)(2,1)} %collective-permute-done.theirs, ...), custom_call_target="tpu_custom_call" | custom-call | tf_op jit(solution)/shard_map/pallas_call | solution.py:133
  41.9 4.6 %collective-permute-start.12 = (f32[4]{0:T(128)S(1)}, f32[4]{0:T(128)S(1)}, u32[]{:S(2)}, u32[]{:S(2)}) collective-permute-start(f32[4]{0:T(128)S(1)} %add.229), channel_id=1, source_target_pairs={{0,8},{2,10},{4,12},{6,14},{8,0},{10,2},{12,4},{14,6},{1,9},{3,11}... | collective-permute-start | bytes 56 | tf_op jit(solution)/shard_map/ppermute | solution.py:71
  48.0 5.8 %shard_map.77 = (f32[1024,128]{1,0:T(8,128)S(1)}, bf16[1024,384]{1,0:T(8,128)(2,1)S(1)}, bf16[1024,384]{1,0:T(8,128)(2,1)S(1)}, bf16[1024,384]{1,0:T(8,128)(2,1)S(1)}) custom-call(s32[6]{0:T(128)S(1)} %stack.64.spots, bf16[512,5120]{1,0:T(8,128)(2,1)S(1)} %bitcast.59, bf16[512,5120]{1,0:T(8,128)(2,1)} %collective-permute-done.theirs, ...), custom_call_target="tpu_custom_call" | custom-call | tf_op jit(solution)/shard_map/pallas_call | solution.py:133
  54.9 2.4 %collective-permute-done.10.refs_0_ = bf16[320,1024]{1,0:T(8,128)(2,1)S(1)} collective-permute-done((bf16[320,1024]{1,0:T(8,128)(2,1)}, bf16[320,1024]{1,0:T(8,128)(2,1)S(1)}, u32[]{:S(2)}, u32[]{:S(2)}) %collective-permute-start.10) | collective-permute-done | bytes 655392 | tf_op jit(solution)/shard_map/ppermute | solution.py:58
  58.3 4.4 %shard_map.78 = (f32[1024,128]{1,0:T(8,128)S(1)}, bf16[1024,384]{1,0:T(8,128)(2,1)S(1)}, bf16[1024,384]{1,0:T(8,128)(2,1)S(1)}) custom-call(s32[4]{0:T(128)S(1)} %pad_add_fusion.spots, bf16[512,5120]{1,0:T(8,128)(2,1)S(1)} %bitcast.60, bf16[512,5120]{1,0:T(8,128)(2,1)} %collective-permute-done.theirs, bf16[512,1024]{1,0:T(8,128)(2,1)S(1)} %bitcast.64, ...), custom_call_target="tpu_custom_call" | custom-call | tf_op jit(solution)/shard_map/pallas_call | solution.py:133
  68.2 1.2 collective-permute-start.14
  74.9 5.1 %collective-permute-done.14 = bf16[320,1024]{1,0:T(8,128)(2,1)S(1)} collective-permute-done((bf16[320,1024]{1,0:T(8,128)(2,1)S(1)}, bf16[320,1024]{1,0:T(8,128)(2,1)S(1)}, u32[]{:S(2)}, u32[]{:S(2)}) %collective-permute-start.14) | collective-permute-done | bytes 655392 | tf_op jit(solution)/shard_map/ppermute | solution.py:67
  86.4 5.4 %collective-permute-done.18 = bf16[320,1024]{1,0:T(8,128)(2,1)S(1)} collective-permute-done((bf16[320,1024]{1,0:T(8,128)(2,1)S(1)}, bf16[320,1024]{1,0:T(8,128)(2,1)S(1)}, u32[]{:S(2)}, u32[]{:S(2)}) %collective-permute-start.18) | collective-permute-done | bytes 655392 | tf_op jit(solution)/shard_map/ppermute | solution.py:58
  91.8 2.4 %collective-permute-done.16 = bf16[320,1024]{1,0:T(8,128)(2,1)S(1)} collective-permute-done((bf16[320,1024]{1,0:T(8,128)(2,1)S(1)}, bf16[320,1024]{1,0:T(8,128)(2,1)S(1)}, u32[]{:S(2)}, u32[]{:S(2)}) %collective-permute-start.16) | collective-permute-done | bytes 655392 | tf_op jit(solution)/shard_map/ppermute | solution.py:38
  94.6 1.3 fusion.3
  97.4 10.5 %collective-permute-done.20 = bf16[320,1024]{1,0:T(8,128)(2,1)S(1)} collective-permute-done((bf16[320,1024]{1,0:T(8,128)(2,1)}, bf16[320,1024]{1,0:T(8,128)(2,1)S(1)}, u32[]{:S(2)}, u32[]{:S(2)}) %collective-permute-start.20) | collective-permute-done | bytes 655392 | tf_op jit(solution)/shard_map/ppermute | solution.py:49
  108.5 1.5 %fusion.21 = (bf16[320,1024]{1,0:T(8,128)(2,1)S(1)}, f32[320,1024]{1,0:T(8,128)S(1)}) fusion(bf16[320,1024]{1,0:T(8,128)(2,1)S(1)} %collective-permute-done.20, bf16[320,1024]{1,0:T(8,128)(2,1)} %collective-permute-done.19, f32[384,1024]{1,0:T(8,128)S(1)} %fusion.31, pred[]{:T(512)S(6)} %eq.40), kind=kLoop, calls=%fused_computation.56 | loop fusion | flops 1966080 | bytes 5898241 | tf_op jit(solution)/shard_map/convert_element_type | solution.py:267
  110.9 1.4 collective-permute-start.26
  112.3 1.4 %collective-permute-start.25 = (bf16[320,128]{1,0:T(8,128)(2,1)S(1)}, bf16[320,128]{1,0:T(8,128)(2,1)S(1)}, u32[]{:S(2)}, u32[]{:S(2)}) collective-permute-start(bf16[320,128]{1,0:T(8,128)(2,1)S(1)} %get-tuple-element.58), channel_id=1, source_target_pairs={{0,12},{2,14},{4,0},{6,2},{8,4},{10,6},{12,8},{14,10},{1,13},{3,15... | collective-permute-start | bytes 245768 | tf_op jit(solution)/shard_map/ppermute | solution.py:75
  113.7 2.7 %collective-permute-start.24 = (bf16[320,128]{1,0:T(8,128)(2,1)S(1)}, bf16[320,128]{1,0:T(8,128)(2,1)S(1)}, u32[]{:S(2)}, u32[]{:S(2)}) collective-permute-start(bf16[320,128]{1,0:T(8,128)(2,1)S(1)} %get-tuple-element.59), channel_id=1, source_target_pairs={{0,4},{2,6},{4,8},{6,10},{8,12},{10,14},{12,0},{14,2},{1,5},{3,7},... | collective-permute-start | bytes 245768 | tf_op jit(solution)/shard_map/ppermute | solution.py:75
  116.4 3.1 %collective-permute-start.23 = (bf16[320,128]{1,0:T(8,128)(2,1)S(1)}, bf16[320,128]{1,0:T(8,128)(2,1)S(1)}, u32[]{:S(2)}, u32[]{:S(2)}) collective-permute-start(bf16[320,128]{1,0:T(8,128)(2,1)S(1)} %get-tuple-element.60), channel_id=1, source_target_pairs={{0,10},{2,12},{4,14},{6,0},{8,2},{10,4},{12,6},{14,8},{1,11},{3,13... | collective-permute-start | bytes 245768 | tf_op jit(solution)/shard_map/ppermute | solution.py:75
  119.5 1.9 %collective-permute-start.22 = (bf16[320,128]{1,0:T(8,128)(2,1)S(1)}, bf16[320,128]{1,0:T(8,128)(2,1)S(1)}, u32[]{:S(2)}, u32[]{:S(2)}) collective-permute-start(bf16[320,128]{1,0:T(8,128)(2,1)S(1)} %get-tuple-element.61), channel_id=1, source_target_pairs={{0,6},{2,8},{4,10},{6,12},{8,14},{10,0},{12,2},{14,4},{1,7},{3,9},... | collective-permute-start | bytes 245768 | tf_op jit(solution)/shard_map/ppermute | solution.py:75
  121.4 1.5 %collective-permute-start.21 = (bf16[320,128]{1,0:T(8,128)(2,1)S(1)}, bf16[320,128]{1,0:T(8,128)(2,1)S(1)}, u32[]{:S(2)}, u32[]{:S(2)}) collective-permute-start(bf16[320,128]{1,0:T(8,128)(2,1)S(1)} %get-tuple-element.55), channel_id=1, source_target_pairs={{0,8},{2,10},{4,12},{6,14},{8,0},{10,2},{12,4},{14,6},{1,9},{3,11}... | collective-permute-start | bytes 245768 | tf_op jit(solution)/shard_map/ppermute | solution.py:75
  123.0 2.4 %collective-permute-done.23 = bf16[320,128]{1,0:T(8,128)(2,1)S(1)} collective-permute-done((bf16[320,128]{1,0:T(8,128)(2,1)S(1)}, bf16[320,128]{1,0:T(8,128)(2,1)S(1)}, u32[]{:S(2)}, u32[]{:S(2)}) %collective-permute-start.23) | collective-permute-done | bytes 81952 | tf_op jit(solution)/shard_map/ppermute | solution.py:75
  125.4 7.0 %collective-permute-done.22 = bf16[320,128]{1,0:T(8,128)(2,1)S(1)} collective-permute-done((bf16[320,128]{1,0:T(8,128)(2,1)S(1)}, bf16[320,128]{1,0:T(8,128)(2,1)S(1)}, u32[]{:S(2)}, u32[]{:S(2)}) %collective-permute-start.22) | collective-permute-done | bytes 81952 | tf_op jit(solution)/shard_map/ppermute | solution.py:75
  133.2 6.2 %collective-permute-done.28 = f32[320,128]{1,0:T(8,128)S(1)} collective-permute-done((f32[320,128]{1,0:T(8,128)S(1)}, f32[320,128]{1,0:T(8,128)S(1)}, u32[]{:S(2)}, u32[]{:S(2)}) %collective-permute-start.28) | collective-permute-done | bytes 163872 | tf_op jit(solution)/shard_map/ppermute | solution.py:79
  (129 shorter events, 35.1 us)
Async XLA Ops:
  0.0 28.8 %collective-permute-start = (bf16[512,5120]{1,0:T(8,128)(2,1)}, bf16[512,5120]{1,0:T(8,128)(2,1)}, u32[]{:S(2)}, u32[]{:S(2)}) collective-permute-start(bf16[512,5120]{1,0:T(8,128)(2,1)} %bitcast.57), channel_id=1, source_target_pairs={{0,16},{16,0},{32,48},{48,32},{64,80},{80,64},{96,112},{112,96},{1... | collective-permute-start | bytes 15728648 | tf_op jit(solution)/shard_map/ppermute | solution.py:33
  2.9 6.4 %collective-permute-start.4 = (f32[4,512]{1,0:T(4,128)S(1)}, f32[4,512]{1,0:T(4,128)S(1)}, u32[]{:S(2)}, u32[]{:S(2)}) collective-permute-start(f32[4,512]{1,0:T(4,128)S(1)} %pad_maximum_fusion.1), channel_id=1, source_target_pairs={{0,16},{16,0},{32,48},{48,32},{64,80},{80,64},{96,112},{112,96},{1... | collective-permute-start | bytes 24584 | tf_op jit(solution)/shard_map/ppermute | solution.py:33
  3.5 11.2 %collective-permute-start.2 = (bf16[320,1024]{1,0:T(8,128)(2,1)}, bf16[320,1024]{1,0:T(8,128)(2,1)S(1)}, u32[]{:S(2)}, u32[]{:S(2)}) collective-permute-start(bf16[320,1024]{1,0:T(8,128)(2,1)} %refs_0_.1), channel_id=1, source_target_pairs={{0,129},{1,128},{16,144},{17,145},{32,161},{33,160},{48,176},{49,1... | collective-permute-start | bytes 1966088 | tf_op jit(solution)/shard_map/ppermute | solution.py:67
  6.3 11.4 %collective-permute-start.3 = (bf16[320,1024]{1,0:T(8,128)(2,1)}, bf16[320,1024]{1,0:T(8,128)(2,1)S(1)}, u32[]{:S(2)}, u32[]{:S(2)}) collective-permute-start(bf16[320,1024]{1,0:T(8,128)(2,1)} %refs_0_.1), channel_id=1, source_target_pairs={{32,0},{50,2},{36,4},{54,6},{40,8},{58,10},{44,12},{62,14},{112,16... | collective-permute-start | bytes 1966088 | tf_op jit(solution)/shard_map/ppermute | solution.py:49
  9.3 19.5 %collective-permute-start.1 = (bf16[512,1024]{1,0:T(8,128)(2,1)}, bf16[512,1024]{1,0:T(8,128)(2,1)S(1)}, u32[]{:S(2)}, u32[]{:S(2)}) collective-permute-start(bf16[512,1024]{1,0:T(8,128)(2,1)} %bitcast.61), channel_id=1, source_target_pairs={{0,16},{16,0},{32,48},{48,32},{64,80},{80,64},{96,112},{112,96},{1... | collective-permute-start | bytes 3145736 | tf_op jit(solution)/shard_map/ppermute | solution.py:33
  10.1 3.6 %collective-permute-start.5 = (f32[4]{0:T(128)S(1)}, f32[4]{0:T(128)S(1)}, u32[]{:S(2)}, u32[]{:S(2)}) collective-permute-start(f32[4]{0:T(128)S(1)} %pad_maximum_fusion.2), channel_id=1, source_target_pairs={{0,2},{2,0},{4,6},{6,4},{8,10},{10,8},{12,14},{14,12},{1,3},{3,1},... | collective-permute-start | bytes 56 | tf_op jit(solution)/shard_map/ppermute | solution.py:71
  17.7 24.2 %collective-permute-start.6 = (bf16[320,1024]{1,0:T(8,128)(2,1)S(1)}, bf16[320,1024]{1,0:T(8,128)(2,1)}, u32[]{:S(2)}, u32[]{:S(2)}) collective-permute-start(bf16[320,1024]{1,0:T(8,128)(2,1)S(1)} %collective-permute-done.3.refs_2_), channel_id=1, source_target_pairs={{0,129},{1,128},{16,144},{17,145},{32,161},{33,160},{48,176},{49,1... | collective-permute-start | bytes 1966088 | tf_op jit(solution)/shard_map/ppermute | solution.py:67
  19.2 22.7 %collective-permute-start.7 = (bf16[320,1024]{1,0:T(8,128)(2,1)S(1)}, bf16[320,1024]{1,0:T(8,128)(2,1)}, u32[]{:S(2)}, u32[]{:S(2)}) collective-permute-start(bf16[320,1024]{1,0:T(8,128)(2,1)S(1)} %collective-permute-done.3.refs_2_), channel_id=1, source_target_pairs={{0,96},{16,48},{32,0},{48,80},{64,32},{80,112},{96,64},{112,16},{1... | collective-permute-start | bytes 1966088 | tf_op jit(solution)/shard_map/ppermute | solution.py:38
  22.2 4.4 %collective-permute-start.9 = (f32[4]{0:T(128)S(1)}, f32[4]{0:T(128)S(1)}, u32[]{:S(2)}, u32[]{:S(2)}) collective-permute-start(f32[4]{0:T(128)S(1)} %fusion.49), channel_id=1, source_target_pairs={{0,4},{2,6},{4,0},{6,2},{8,12},{10,14},{12,8},{14,10},{1,5},{3,7},... | collective-permute-start | bytes 56 | tf_op jit(solution)/shard_map/ppermute | solution.py:71
  26.6 15.3 %collective-permute-start.8 = (bf16[320,1024]{1,0:T(8,128)(2,1)S(1)}, bf16[320,1024]{1,0:T(8,128)(2,1)}, u32[]{:S(2)}, u32[]{:S(2)}) collective-permute-start(bf16[320,1024]{1,0:T(8,128)(2,1)S(1)} %collective-permute-done.3.refs_2_), channel_id=1, source_target_pairs={{0,2},{2,0},{4,6},{6,4},{8,10},{10,8},{12,14},{14,12},{16,30},{18,... | collective-permute-start | bytes 1966088 | tf_op jit(solution)/shard_map/ppermute | solution.py:58
  34.8 13.2 %copy-start.1 = (bf16[1,2,256,5120]{3,2,1,0:T(8,128)(2,1)S(1)}, bf16[1,2,256,5120]{3,2,1,0:T(8,128)(2,1)}, u32[]{:S(2)}) copy-start(bf16[1,2,256,5120]{3,2,1,0:T(8,128)(2,1)} %param.7) | copy-start | bytes 15728644
  34.8 13.2 %copy-start.3 = (bf16[1,2,256,1024]{3,2,1,0:T(8,128)(2,1)S(1)}, bf16[1,2,256,1024]{3,2,1,0:T(8,128)(2,1)}, u32[]{:S(2)}) copy-start(bf16[1,2,256,1024]{3,2,1,0:T(8,128)(2,1)} %param.9) | copy-start | bytes 3145732
  41.9 12.7 %collective-permute-start.12 = (f32[4]{0:T(128)S(1)}, f32[4]{0:T(128)S(1)}, u32[]{:S(2)}, u32[]{:S(2)}) collective-permute-start(f32[4]{0:T(128)S(1)} %add.229), channel_id=1, source_target_pairs={{0,8},{2,10},{4,12},{6,14},{8,0},{10,2},{12,4},{14,6},{1,9},{3,11}... | collective-permute-start | bytes 56 | tf_op jit(solution)/shard_map/ppermute | solution.py:71
  46.5 10.8 %collective-permute-start.10 = (bf16[320,1024]{1,0:T(8,128)(2,1)}, bf16[320,1024]{1,0:T(8,128)(2,1)S(1)}, u32[]{:S(2)}, u32[]{:S(2)}) collective-permute-start(bf16[320,1024]{1,0:T(8,128)(2,1)} %collective-permute-done.6.refs_1_), channel_id=1, source_target_pairs={{0,2},{2,0},{4,6},{6,4},{8,10},{10,8},{12,14},{14,12},{16,30},{18,... | collective-permute-start | bytes 1966088 | tf_op jit(solution)/shard_map/ppermute | solution.py:58
  47.5 10.8 %collective-permute-start.11 = (bf16[320,1024]{1,0:T(8,128)(2,1)}, bf16[320,1024]{1,0:T(8,128)(2,1)S(1)}, u32[]{:S(2)}, u32[]{:S(2)}) collective-permute-start(bf16[320,1024]{1,0:T(8,128)(2,1)} %collective-permute-done.7.refs_2_), channel_id=1, source_target_pairs={{0,129},{1,128},{16,144},{17,145},{32,161},{33,160},{48,176},{49,1... | collective-permute-start | bytes 1966088 | tf_op jit(solution)/shard_map/ppermute | solution.py:67
  64.7 1.3 collective-permute-start.13
  66.4 18.1 %copy-start.21 = (bf16[1024,1024]{1,0:T(8,128)(2,1)}, bf16[1024,1024]{1,0:T(8,128)(2,1)S(1)}, u32[]{:S(2)}) copy-start(bf16[1024,1024]{1,0:T(8,128)(2,1)S(1)} %multiply_convert_fusion) | copy-start | bytes 6291460
  68.2 11.9 %collective-permute-start.14 = (bf16[320,1024]{1,0:T(8,128)(2,1)S(1)}, bf16[320,1024]{1,0:T(8,128)(2,1)S(1)}, u32[]{:S(2)}, u32[]{:S(2)}) collective-permute-start(bf16[320,1024]{1,0:T(8,128)(2,1)S(1)} %fusion.12), channel_id=1, source_target_pairs={{0,128},{1,129},{16,145},{17,144},{32,160},{33,161},{48,177},{49,1... | collective-permute-start | bytes 1966088 | tf_op jit(solution)/shard_map/ppermute | solution.py:67
  70.5 10.7 %collective-permute-start.15 = (bf16[320,1024]{1,0:T(8,128)(2,1)S(1)}, bf16[320,1024]{1,0:T(8,128)(2,1)S(1)}, u32[]{:S(2)}, u32[]{:S(2)}) collective-permute-start(bf16[320,1024]{1,0:T(8,128)(2,1)S(1)} %fusion.11), channel_id=1, source_target_pairs={{0,2},{2,0},{4,6},{6,4},{8,10},{10,8},{12,14},{14,12},{16,30},{18,... | collective-permute-start | bytes 1966088 | tf_op jit(solution)/shard_map/ppermute | solution.py:58
  81.2 10.6 %collective-permute-start.18 = (bf16[320,1024]{1,0:T(8,128)(2,1)S(1)}, bf16[320,1024]{1,0:T(8,128)(2,1)S(1)}, u32[]{:S(2)}, u32[]{:S(2)}) collective-permute-start(bf16[320,1024]{1,0:T(8,128)(2,1)S(1)} %fusion.13), channel_id=1, source_target_pairs={{0,2},{2,0},{4,6},{6,4},{8,10},{10,8},{12,14},{14,12},{16,30},{18,... | collective-permute-start | bytes 1966088 | tf_op jit(solution)/shard_map/ppermute | solution.py:58
  82.3 11.9 %collective-permute-start.16 = (bf16[320,1024]{1,0:T(8,128)(2,1)S(1)}, bf16[320,1024]{1,0:T(8,128)(2,1)S(1)}, u32[]{:S(2)}, u32[]{:S(2)}) collective-permute-start(bf16[320,1024]{1,0:T(8,128)(2,1)S(1)} %fusion.9), channel_id=1, source_target_pairs={{0,32},{16,112},{32,64},{48,16},{64,96},{80,48},{96,0},{112,80},{1... | collective-permute-start | bytes 1966088 | tf_op jit(solution)/shard_map/ppermute | solution.py:38
  82.7 11.9 %collective-permute-start.17 = (bf16[320,1024]{1,0:T(8,128)(2,1)S(1)}, bf16[320,1024]{1,0:T(8,128)(2,1)S(1)}, u32[]{:S(2)}, u32[]{:S(2)}) collective-permute-start(bf16[320,1024]{1,0:T(8,128)(2,1)S(1)} %fusion.7), channel_id=1, source_target_pairs={{0,128},{1,129},{16,145},{17,144},{32,160},{33,161},{48,177},{49,1... | collective-permute-start | bytes 1966088 | tf_op jit(solution)/shard_map/ppermute | solution.py:67
  95.9 12.0 %collective-permute-start.20 = (bf16[320,1024]{1,0:T(8,128)(2,1)}, bf16[320,1024]{1,0:T(8,128)(2,1)S(1)}, u32[]{:S(2)}, u32[]{:S(2)}) collective-permute-start(bf16[320,1024]{1,0:T(8,128)(2,1)} %fusion.3), channel_id=1, source_target_pairs={{0,32},{2,50},{4,36},{6,54},{8,40},{10,58},{12,44},{14,62},{16,112... | collective-permute-start | bytes 1966088 | tf_op jit(solution)/shard_map/ppermute | solution.py:49
  96.4 12.1 %collective-permute-start.19 = (bf16[320,1024]{1,0:T(8,128)(2,1)}, bf16[320,1024]{1,0:T(8,128)(2,1)}, u32[]{:S(2)}, u32[]{:S(2)}) collective-permute-start(bf16[320,1024]{1,0:T(8,128)(2,1)} %fusion.10), channel_id=1, source_target_pairs={{0,128},{1,129},{16,145},{17,144},{32,160},{33,161},{48,177},{49,1... | collective-permute-start | bytes 1966088 | tf_op jit(solution)/shard_map/ppermute | solution.py:67
  110.2 9.4 %collective-permute-start.27 = (bf16[320,128]{1,0:T(8,128)(2,1)S(1)}, bf16[320,128]{1,0:T(8,128)(2,1)S(1)}, u32[]{:S(2)}, u32[]{:S(2)}) collective-permute-start(bf16[320,128]{1,0:T(8,128)(2,1)S(1)} %get-tuple-element.56), channel_id=1, source_target_pairs={{0,14},{2,0},{4,2},{6,4},{8,6},{10,8},{12,10},{14,12},{1,15},{3,1}... | collective-permute-start | bytes 245768 | tf_op jit(solution)/shard_map/ppermute | solution.py:75
  110.9 10.5 %collective-permute-start.26 = (bf16[320,128]{1,0:T(8,128)(2,1)S(1)}, bf16[320,128]{1,0:T(8,128)(2,1)S(1)}, u32[]{:S(2)}, u32[]{:S(2)}) collective-permute-start(bf16[320,128]{1,0:T(8,128)(2,1)S(1)} %get-tuple-element.57), channel_id=1, source_target_pairs={{0,2},{2,4},{4,6},{6,8},{8,10},{10,12},{12,14},{14,0},{1,3},{3,5},... | collective-permute-start | bytes 245768 | tf_op jit(solution)/shard_map/ppermute | solution.py:75
  112.3 10.7 %collective-permute-start.25 = (bf16[320,128]{1,0:T(8,128)(2,1)S(1)}, bf16[320,128]{1,0:T(8,128)(2,1)S(1)}, u32[]{:S(2)}, u32[]{:S(2)}) collective-permute-start(bf16[320,128]{1,0:T(8,128)(2,1)S(1)} %get-tuple-element.58), channel_id=1, source_target_pairs={{0,12},{2,14},{4,0},{6,2},{8,4},{10,6},{12,8},{14,10},{1,13},{3,15... | collective-permute-start | bytes 245768 | tf_op jit(solution)/shard_map/ppermute | solution.py:75
  113.7 9.2 %collective-permute-start.24 = (bf16[320,128]{1,0:T(8,128)(2,1)S(1)}, bf16[320,128]{1,0:T(8,128)(2,1)S(1)}, u32[]{:S(2)}, u32[]{:S(2)}) collective-permute-start(bf16[320,128]{1,0:T(8,128)(2,1)S(1)} %get-tuple-element.59), channel_id=1, source_target_pairs={{0,4},{2,6},{4,8},{6,10},{8,12},{10,14},{12,0},{14,2},{1,5},{3,7},... | collective-permute-start | bytes 245768 | tf_op jit(solution)/shard_map/ppermute | solution.py:75
  116.4 9.0 %collective-permute-start.23 = (bf16[320,128]{1,0:T(8,128)(2,1)S(1)}, bf16[320,128]{1,0:T(8,128)(2,1)S(1)}, u32[]{:S(2)}, u32[]{:S(2)}) collective-permute-start(bf16[320,128]{1,0:T(8,128)(2,1)S(1)} %get-tuple-element.60), channel_id=1, source_target_pairs={{0,10},{2,12},{4,14},{6,0},{8,2},{10,4},{12,6},{14,8},{1,11},{3,13... | collective-permute-start | bytes 245768 | tf_op jit(solution)/shard_map/ppermute | solution.py:75
  119.5 12.9 %collective-permute-start.22 = (bf16[320,128]{1,0:T(8,128)(2,1)S(1)}, bf16[320,128]{1,0:T(8,128)(2,1)S(1)}, u32[]{:S(2)}, u32[]{:S(2)}) collective-permute-start(bf16[320,128]{1,0:T(8,128)(2,1)S(1)} %get-tuple-element.61), channel_id=1, source_target_pairs={{0,6},{2,8},{4,10},{6,12},{8,14},{10,0},{12,2},{14,4},{1,7},{3,9},... | collective-permute-start | bytes 245768 | tf_op jit(solution)/shard_map/ppermute | solution.py:75
  121.4 10.9 %collective-permute-start.21 = (bf16[320,128]{1,0:T(8,128)(2,1)S(1)}, bf16[320,128]{1,0:T(8,128)(2,1)S(1)}, u32[]{:S(2)}, u32[]{:S(2)}) collective-permute-start(bf16[320,128]{1,0:T(8,128)(2,1)S(1)} %get-tuple-element.55), channel_id=1, source_target_pairs={{0,8},{2,10},{4,12},{6,14},{8,0},{10,2},{12,4},{14,6},{1,9},{3,11}... | collective-permute-start | bytes 245768 | tf_op jit(solution)/shard_map/ppermute | solution.py:75
  132.5 6.9 %collective-permute-start.28 = (f32[320,128]{1,0:T(8,128)S(1)}, f32[320,128]{1,0:T(8,128)S(1)}, u32[]{:S(2)}, u32[]{:S(2)}) collective-permute-start(f32[320,128]{1,0:T(8,128)S(1)} %convert_add_fusion), channel_id=1, source_target_pairs={{0,1},{1,0},{2,3},{3,2},{4,5},{5,4},{6,7},{7,6},{8,9},{9,8},{10,11... | collective-permute-start | bytes 491528 | tf_op jit(solution)/shard_map/ppermute | solution.py:79
  (22 other events, 91.1 us)
